TPU v7x, 32 devices: a whole 2x2x4 slice. The times are simulated.
32 devices in a mesh: groups: 2 (over y), seq: 8 (over z, x), batch: 2 (over core).
Axes of the slice: x: 2, y: 2, z: 4, core: 2. Of those that a mesh axis runs over, the one named last changes fastest.
Arguments:
- x_in: bfloat16 [4, 512, 2560], P(('groups', 'batch'), 'seq'), parts along dimension 0, may hold values from -6 to 6
- b_in: bfloat16 [4, 512, 128], P(('groups', 'batch'), 'seq'), parts along dimension 0, may hold values from -0.1875 to 0.1875
- c_in: bfloat16 [4, 512, 128], P(('groups', 'batch'), 'seq'), parts along dimension 0, may hold values from -6 to 6
- log_decay: float32 [4, 40, 512], P(('groups', 'batch'), None, 'seq'), parts along dimension 0, may hold values from -0.8 to 0, as said below
- skip: float32 [40], replicated, may hold values from 0.5 to 4
- norm_gain: float32 [2560], replicated, may hold values from 0.1 to 1.9
- queries: bfloat16 [4, 512, 512], P(('groups', 'batch'), 'seq'), parts along dimension 0, may hold values from -60 to 60
- keys: bfloat16 [4, 512, 512], P(('groups', 'batch'), 'seq'), parts along dimension 0, may hold values from -4 to 4
Outputs:
- scan_out: bfloat16 [4, 512, 2560], P(('groups', 'batch'), 'seq'), parts along dimension 0
- attended: bfloat16 [4, 512, 512], P(('groups', 'batch'), 'seq'), parts along dimension 0
There are 2 independent parts, one for each index of `groups`. A program takes and returns all parts, laid end to end along the dimension named above; an argument that names none is the same for every part. Nothing has to cross between parts.
Inputs may be any that keep to these rules, and one draw needn't show every extreme that they name: log_decay is never positive.
All inputs are finite; a program needn't handle non-finite values.
Results may differ from a plain program's by a relative error of at most 0.0051.
Values may be sent and summed in bfloat16 or wider, within the bound.
A program may use at most 128 MiB of HBM per device.

v0:
```python
import jax
import jax.numpy as jnp
from jax import lax
from jax.sharding import PartitionSpec as P

SPAN = 64


HIGH = lax.Precision.HIGHEST


def carried_in(part, axis, combine, identity):
    place = lax.axis_index(axis)
    gathered = jax.tree.map(lambda a: lax.all_gather(a, axis), part)
    state = jax.tree.map(lambda a, e: jnp.zeros_like(a) + jnp.asarray(e, a.dtype), part, identity)

    def one(step, state):
        return combine(
            state, jax.tree.map(lambda a: lax.dynamic_index_in_dim(a, step, 0, False), gathered)
        )

    return lax.fori_loop(0, place, one, state)


def attend_heads(q_heads, k_heads, v_heads, head_dim):
    length = q_heads.shape[0]
    heads_here = q_heads.shape[1] // head_dim
    block = min(512, length)
    count = length // block
    scale = head_dim ** (-0.5)
    key_part = k_heads.reshape(length, heads_here, head_dim)
    value_part = v_heads.reshape(length, heads_here, head_dim)

    def one_block(index):
        start = index * block
        part = lax.dynamic_slice_in_dim(q_heads, start, block, 0).reshape(
            block, heads_here, head_dim
        )
        scores = (
            jnp.einsum("qhd,khd->hqk", part, key_part, preferred_element_type=jnp.float32) * scale
        )
        rows = start + jnp.arange(block, dtype=jnp.int32)
        cols = jnp.arange(length, dtype=jnp.int32)
        mask = cols[None, None, :] <= rows[None, :, None]
        scores = jnp.where(mask, scores, -jnp.inf)
        top = jnp.max(scores, axis=-1, keepdims=True)
        probs = jnp.exp(scores - top)
        total = jnp.sum(probs, axis=-1, keepdims=True)
        mixed = jnp.einsum(
            "hqk,khd->qhd",
            probs.astype(jnp.bfloat16),
            value_part,
            preferred_element_type=jnp.float32,
        )
        mixed = mixed / jnp.transpose(total, (1, 0, 2))
        return mixed.astype(jnp.bfloat16).reshape(block, heads_here * head_dim)

    blocks = lax.map(one_block, jnp.arange(count, dtype=jnp.int32))
    return blocks.reshape(length, heads_here * head_dim)


def local(x_in, b_in, c_in, log_decay, skip, norm_gain, queries, keys):
    tok = x_in.shape[1]
    width = x_in.shape[2]
    heads = log_decay.shape[1]
    head_dim = width // heads
    state = b_in.shape[2]
    att_width = queries.shape[2]
    nchunk = tok // SPAN
    xr = x_in[0].astype(jnp.float32).reshape(nchunk, SPAN, heads, head_dim)
    br = b_in[0].astype(jnp.float32).reshape(nchunk, SPAN, state)
    cr = c_in[0].astype(jnp.float32).reshape(nchunk, SPAN, state)
    rates = log_decay[0].reshape(heads, nchunk, SPAN).transpose(1, 0, 2)
    cums = jnp.cumsum(rates, axis=-1)
    lower = jnp.arange(SPAN)[:, None] >= jnp.arange(SPAN)[None, :]
    inner = jnp.einsum("ctn,csn->cts", cr, br, precision=HIGH)
    weights = jnp.where(lower, jnp.exp(cums[..., :, None] - cums[..., None, :]), 0.0)
    weighted = inner[:, None, :, :] * weights
    intra = jnp.einsum("chts,cshp->cthp", weighted, xr, precision=HIGH)

    def advance(carry, pieces):
        xs, bs, cs_, cum = pieces
        reach = jnp.transpose(jnp.exp(cum), (1, 0))[:, :, None]
        readout = reach * jnp.einsum("tn,hpn->thp", cs_, carry, precision=HIGH)
        tail = jnp.exp(cum[:, -1:] - cum)
        fresh = jnp.einsum("hs,shp,sn->hpn", tail, xs, bs, precision=HIGH)
        carry = jnp.exp(cum[:, -1])[:, None, None] * carry + fresh
        return (carry, readout)

    empty = jnp.zeros((heads, head_dim, state), jnp.float32)
    final, carried = lax.scan(advance, empty, (xr, br, cr, cums))
    total_decay = jnp.sum(log_decay[0], axis=1)

    def link(earlier, later):
        return (jnp.exp(later[1])[:, None, None] * earlier[0] + later[0], earlier[1] + later[1])

    incoming, _ = carried_in(
        (final, total_decay), "seq", link, (empty, jnp.zeros((heads,), jnp.float32))
    )
    ends = cums[:, :, -1]
    offsets = jnp.cumsum(ends, axis=0) - ends
    reach_all = jnp.transpose(jnp.exp(cums + offsets[:, :, None]), (0, 2, 1))[..., None]
    late = reach_all * jnp.einsum("ctn,hpn->cthp", cr, incoming, precision=HIGH)
    outputs = intra + carried + late + skip[None, None, :, None] * xr
    y_rows = outputs.reshape(tok, heads, head_dim)
    mean_sq = jnp.mean(y_rows * y_rows, axis=-1, keepdims=True)
    normed = y_rows * lax.rsqrt(mean_sq + 1e-05) * norm_gain.reshape(heads, head_dim)
    scan_rows = normed.astype(jnp.bfloat16).reshape(tok, width)
    values = scan_rows[:, :att_width]
    q_heads, k_heads, v_heads = (
        lax.all_to_all(queries[0], "seq", split_axis=1, concat_axis=0, tiled=True),
        lax.all_to_all(keys[0], "seq", split_axis=1, concat_axis=0, tiled=True),
        lax.all_to_all(values, "seq", split_axis=1, concat_axis=0, tiled=True),
    )
    attended_heads = attend_heads(q_heads, k_heads, v_heads, head_dim)
    attended_rows = lax.all_to_all(attended_heads, "seq", split_axis=0, concat_axis=1, tiled=True)
    return (scan_rows[None], attended_rows[None])


def solution(mesh):
    return jax.shard_map(
        local,
        mesh=mesh,
        in_specs=(
            P(("groups", "batch"), "seq", None),
            P(("groups", "batch"), "seq", None),
            P(("groups", "batch"), "seq", None),
            P(("groups", "batch"), None, "seq"),
            P(),
            P(),
            P(("groups", "batch"), "seq", None),
            P(("groups", "batch"), "seq", None),
        ),
        out_specs=(P(("groups", "batch"), "seq", None), P(("groups", "batch"), "seq", None)),
        check_vma=False,
    )
```

profile of v0, /device:TPU:0, one launch (start us, length us, event | category | flops | bytes accessed | tf_op | source)
XLA Modules:
  0.0 214.6 jit_solution(10238974393252425942)
XLA Ops:
  7.2 0.9 reduce_window_sum.17
  8.5 1.3 copy.48
  9.8 1.9 convolution_add_fusion
  11.8 0.8 reshape.273
  12.6 7.3 %all-to-all-start.1 = ((bf16[8,2,2048]{2,1,0:T(2,128)(2,1)}), bf16[8,2,2048]{2,1,0:T(2,128)(2,1)S(1)}, u32[]{:S(2)}, u32[]{:S(2)}) async-start(bf16[8,2,2048]{2,1,0:T(2,128)(2,1)} %reshape.273), calls=%async_computation.1 | async-start | bytes 131072 | tf_op jit(solution)/shard_map/all_to_all | solution.py:111
  20.3 1.8 fusion.1
  22.2 1.3 copy.35
  25.0 22.4 %all-reduce = f32[320]{0:T(512)S(1)} all-reduce(f32[320]{0:T(512)S(1)} %dynamic-update-slice), channel_id=2, replica_groups=mesh['groups'=2,'seq'=8,'batch'=2] {'seq'}, use_global_device_ids=true, to_apply=%add | all-reduce | flops 320 | bytes 2560
  47.6 0.8 reshape.275
  48.5 3.4 %all-to-all-start.2 = ((bf16[8,2,2048]{2,1,0:T(2,128)(2,1)}), bf16[8,2,2048]{2,1,0:T(2,128)(2,1)S(1)}, u32[]{:S(2)}, u32[]{:S(2)}) async-start(bf16[8,2,2048]{2,1,0:T(2,128)(2,1)} %reshape.275), calls=%async_computation.2 | async-start | bytes 131072 | tf_op jit(solution)/shard_map/all_to_all | solution.py:112
  52.2 7.3 %all-to-all-done.2 = bf16[8,2,2048]{2,1,0:T(2,128)(2,1)S(1)} async-done(((bf16[8,2,2048]{2,1,0:T(2,128)(2,1)}), bf16[8,2,2048]{2,1,0:T(2,128)(2,1)S(1)}, u32[]{:S(2)}, u32[]{:S(2)}) %all-to-all-start.2) | async-done | bytes 65568 | tf_op jit(solution)/shard_map/all_to_all | solution.py:112
  59.9 1.3 fusion.39
  61.2 105.7 %all-gather.4.cloned.1.call-done = f32[320,64,128]{2,1,0:T(8,128)} async-done(((f32[40,64,128]{2,1,0:T(8,128)}), f32[320,64,128]{2,1,0:T(8,128)}) %all-gather.4.cloned.1.call-update) | async-done | bytes 10485776 | tf_op jit(solution)/shard_map/all_gather | solution.py:14
  168.8 1.8 multiply_reduce_fusion
  171.1 1.2 mul.148
  172.4 0.9 fusion.29
  173.5 0.8 reshape.271
  174.3 14.0 %all-to-all-start = ((bf16[8,2,2048]{2,1,0:T(2,128)(2,1)}), bf16[8,2,2048]{2,1,0:T(2,128)(2,1)S(1)}, u32[]{:S(2)}, u32[]{:S(2)}) async-start(bf16[8,2,2048]{2,1,0:T(2,128)(2,1)} %reshape.271), calls=%async_computation | async-start | bytes 131072 | tf_op jit(solution)/shard_map/all_to_all | solution.py:113
  188.3 1.4 fusion.17
  190.1 1.2 copy.37
  191.3 3.9 %all-to-all-done = bf16[8,2,2048]{2,1,0:T(2,128)(2,1)S(1)} async-done(((bf16[8,2,2048]{2,1,0:T(2,128)(2,1)}), bf16[8,2,2048]{2,1,0:T(2,128)(2,1)S(1)}, u32[]{:S(2)}, u32[]{:S(2)}) %all-to-all-start) | async-done | bytes 65568 | tf_op jit(solution)/shard_map/all_to_all | solution.py:113
  196.6 3.4 %all-to-all-start.3 = ((bf16[8,2,2048]{2,1,0:T(2,128)(2,1)}), bf16[8,2,2048]{2,1,0:T(2,128)(2,1)S(1)}, u32[]{:S(2)}, u32[]{:S(2)}) async-start(bf16[8,2,2048]{2,1,0:T(2,128)(2,1)} %reshape.277), calls=%async_computation.3 | async-start | bytes 131072 | tf_op jit(solution)/shard_map/all_to_all | solution.py:116
  200.0 0.8 multiply_convert_fusion
  200.8 6.0 %all-to-all-done.3 = bf16[8,2,2048]{2,1,0:T(2,128)(2,1)S(1)} async-done(((bf16[8,2,2048]{2,1,0:T(2,128)(2,1)}), bf16[8,2,2048]{2,1,0:T(2,128)(2,1)S(1)}, u32[]{:S(2)}, u32[]{:S(2)}) %all-to-all-start.3) | async-done | bytes 65568 | tf_op jit(solution)/shard_map/all_to_all | solution.py:116
  (71 shorter events, 8.0 us)
Async XLA Ops:
  7.2 2.6 %copy-start = (bf16[1,64,128]{2,1,0:T(8,128)(2,1)S(1)}, bf16[1,64,128]{2,1,0:T(8,128)(2,1)}, u32[]{:S(2)}) copy-start(bf16[1,64,128]{2,1,0:T(8,128)(2,1)} %param.11) | copy-start | bytes 49156
  7.2 159.7 %all-gather.4.cloned.1.call-start = ((), (), s32[]{:S(2)}) async-start(), calls=%async_computation.4 | async-start | bytes 11796480 | tf_op jit(solution)/shard_map/all_gather | solution.py:14
  9.8 1.9 copy-start.8
  11.7 8.5 %copy-start.6 = (bf16[1,64,128]{2,1,0:T(8,128)(2,1)S(1)}, bf16[1,64,128]{2,1,0:T(8,128)(2,1)}, u32[]{:S(2)}) copy-start(bf16[1,64,128]{2,1,0:T(8,128)(2,1)} %param.12) | copy-start | bytes 49156
  11.7 10.4 %copy-start.7 = (f32[1,40,64]{2,1,0:T(8,128)S(1)}, f32[1,40,64]{2,1,0:T(8,128)}, u32[]{:S(2)}) copy-start(f32[1,40,64]{2,1,0:T(8,128)} %param.13) | copy-start | bytes 30724
  11.7 10.5 %copy-start.5 = (bf16[1,64,2560]{2,1,0:T(8,128)(2,1)S(1)}, bf16[1,64,2560]{2,1,0:T(8,128)(2,1)}, u32[]{:S(2)}) copy-start(bf16[1,64,2560]{2,1,0:T(8,128)(2,1)} %param.10) | copy-start | bytes 983044
  12.6 35.8 %all-to-all-start.1 = ((bf16[8,2,2048]{2,1,0:T(2,128)(2,1)}), bf16[8,2,2048]{2,1,0:T(2,128)(2,1)S(1)}, u32[]{:S(2)}, u32[]{:S(2)}) async-start(bf16[8,2,2048]{2,1,0:T(2,128)(2,1)} %reshape.273), calls=%async_computation.1 | async-start | bytes 131072 | tf_op jit(solution)/shard_map/all_to_all | solution.py:111
  20.3 3.2 %copy-start.12 = (u32[32]{0:T(128)S(1)}, u32[32]{0:T(128)}, u32[]{:S(2)}) copy-start(u32[32]{0:T(128)} %constant.82) | copy-start | bytes 388
  20.3 27.2 %copy-start.9 = (bf16[1,64,512]{2,1,0:T(8,128)(2,1)S(1)}, bf16[1,64,512]{2,1,0:T(8,128)(2,1)}, u32[]{:S(2)}) copy-start(bf16[1,64,512]{2,1,0:T(8,128)(2,1)} %param.17) | copy-start | bytes 196612
  48.5 11.1 %all-to-all-start.2 = ((bf16[8,2,2048]{2,1,0:T(2,128)(2,1)}), bf16[8,2,2048]{2,1,0:T(2,128)(2,1)S(1)}, u32[]{:S(2)}, u32[]{:S(2)}) async-start(bf16[8,2,2048]{2,1,0:T(2,128)(2,1)} %reshape.275), calls=%async_computation.2 | async-start | bytes 131072 | tf_op jit(solution)/shard_map/all_to_all | solution.py:112
  167.1 1.3 copy-start.1
  167.1 1.7 copy-start.2
  167.1 1.7 copy-start.11
  171.1 1.3 slice-start
  174.3 20.9 %all-to-all-start = ((bf16[8,2,2048]{2,1,0:T(2,128)(2,1)}), bf16[8,2,2048]{2,1,0:T(2,128)(2,1)S(1)}, u32[]{:S(2)}, u32[]{:S(2)}) async-start(bf16[8,2,2048]{2,1,0:T(2,128)(2,1)} %reshape.271), calls=%async_computation | async-start | bytes 131072 | tf_op jit(solution)/shard_map/all_to_all | solution.py:113
  190.1 5.3 %copy-start.3 = (f32[512,512]{0,1:T(8,128)S(1)}, f32[512,512]{0,1:T(8,128)}, u32[]{:S(2)}) copy-start(f32[512,512]{0,1:T(8,128)} %get-tuple-element.100) | copy-start | bytes 3145732
  191.3 8.7 %copy-start.4 = (f32[1,64,2560]{2,1,0:T(8,128)S(1)}, f32[1,64,2560]{2,1,0:T(8,128)}, u32[]{:S(2)}) copy-start(f32[1,64,2560]{2,1,0:T(8,128)} %copy.37) | copy-start | bytes 1966084
  191.3 8.7 %copy-start.10 = (f32[2560]{0:T(1024)S(1)}, f32[2560]{0:T(1024)}, u32[]{:S(2)}) copy-start(f32[2560]{0:T(1024)} %param.15) | copy-start | bytes 30724
  196.6 10.2 %all-to-all-start.3 = ((bf16[8,2,2048]{2,1,0:T(2,128)(2,1)}), bf16[8,2,2048]{2,1,0:T(2,128)(2,1)S(1)}, u32[]{:S(2)}, u32[]{:S(2)}) async-start(bf16[8,2,2048]{2,1,0:T(2,128)(2,1)} %reshape.277), calls=%async_computation.3 | async-start | bytes 131072 | tf_op jit(solution)/shard_map/all_to_all | solution.py:116
Sparse Core Ops, SparseCore 0:
  11.8 155.0 all-gather.3
where the time goes:
time: 215 us
  waiting for transfers between devices  123 us (57%)
  starting transfers between devices  28 us (13%)
  blocking collectives  22.4 us (10%)
  between operations  15.1 us (7%)
  local copies, waits for them, and re-layouts  13.7 us (6%)
  matrix products  7.9 us (4%)
  other arithmetic  4.59 us (2%)
    all_gather x1, waiting for transfers between devices, carried_in(): gathered = jax.tree.map(lambda a: lax.all_gather(a, axis), part)  106 us
    unnamed x1, blocking collectives  22.4 us
    all_to_all x1, starting transfers between devices, local(): lax.all_to_all(values, 'seq', split_axis=1, concat_axis=0, tiled=True)  14 us
    all_to_all x1, waiting for transfers between devices, local(): lax.all_to_all(keys[0], 'seq', split_axis=1, concat_axis=0, tiled=True)  7.29 us
    all_to_all x1, starting transfers between devices, local(): lax.all_to_all(queries[0], 'seq', split_axis=1, concat_axis=0, tiled=True)  7.25 us
    unnamed x41, local copies, waits for them, and re-layouts  6.65 us
    all_to_all x1, waiting for transfers between devices, local(): lax.all_to_all(attended_heads, 'seq', split_axis=0, concat_axis=1, tiled=...  6 us
  transfers between devices with their start and end apart: 5, of which 4 were waited for; matrix products, arithmetic and copies ran while one was open for 6% of the time, Pallas kernels for 0%

commit v1 on v0

v1 whole, which is shorter than its diff:
```python
import functools
import math
import jax
import jax.numpy as jnp
from jax import lax
from jax.sharding import PartitionSpec as P
from jax.experimental import pallas as pl
from jax.experimental.pallas import tpu as pltpu

F32 = jnp.float32
BF16 = jnp.bfloat16
HIGH = lax.Precision.HIGHEST
LOG2E = math.log2(math.e)
MESH = pl.DeviceIdType.MESH
BC, LD, QK, ATT, FIXED = 0, 1, 2, 3, 4


def lanes(a, b):
    return jnp.concatenate([a, b], axis=1)


def rows(parts):
    return jnp.concatenate(parts, axis=0)


def kernel(n, tok, heads, dim, per, blk,
           x_ref, b_ref, c_ref, ld_ref, skip_ref, gain_ref, q_ref, k_ref,
           out_ref, att_ref,
           xs, xr, qks, qkr, bcs, bcr, lds, ldr, ys, yr, ats, atr, inner, send, recv):
    me = lax.axis_index("seq")
    half = tok // 2
    slots = xs.shape[1]
    length = n * tok
    nblk = length // blk

    barrier = pltpu.get_barrier_semaphore()

    def greet(k, _):
        pl.semaphore_signal(barrier, inc=1, device_id={"seq": lax.rem(me + k, n)}, device_id_type=MESH)
        return 0

    lax.fori_loop(1, n, greet, 0)

    def copy(src, dst, row, k):
        return pltpu.make_async_remote_copy(
            src_ref=src, dst_ref=dst, send_sem=send.at[row, k], recv_sem=recv.at[row, k],
            device_id={"seq": lax.rem(me + k, n)}, device_id_type=MESH)

    def to(k):
        return lax.rem(me + k, n)

    def each(fn):
        def body(k, _):
            fn(k)
            return 0
        lax.fori_loop(1, n, body, 0)

    bc_copy = lambda k: copy(bcs, bcr.at[me], BC, k)
    ld_copy = lambda k: copy(lds.at[to(k)], ldr.at[me], LD, k)
    qk_copy = lambda k: copy(qks.at[to(k)], qkr.at[me], QK, k)
    att_copy = lambda k: copy(ats.at[to(k)], atr.at[me], ATT, k)
    x_copy = lambda slot: lambda k: copy(xs.at[to(k), slot], xr.at[me, slot], FIXED + slot, k)
    y_copy = lambda slot: lambda k: copy(ys.at[to(k), slot], yr.at[me, slot], FIXED + slots + slot, k)
    start = lambda mk: each(lambda k: mk(k).start())
    arrive = lambda mk: each(lambda k: mk(k).wait_recv())
    left = lambda mk: each(lambda k: mk(k).wait_send())

    bcs[0:tok] = b_ref[0]
    bcs[tok:] = c_ref[0]
    bcr[me] = bcs[...]
    upper = (lax.broadcasted_iota(jnp.int32, (tok, tok), 0)
             <= lax.broadcasted_iota(jnp.int32, (tok, tok), 1)).astype(F32)
    sums = jnp.dot(ld_ref[0], upper, precision=HIGH, preferred_element_type=F32) * LOG2E
    lds[...] = jnp.zeros_like(lds)
    for slot in range(slots):
        count = min(n, heads - slot * n)
        lds[0:count, slot, 0:tok] = sums[slot * n : slot * n + count]
    ldr[me] = lds[me]

    def pack(src, head_of, store):
        for p in range(src.shape[2] // (2 * dim)):
            t = src[0, :, p * 2 * dim : (p + 1) * 2 * dim]
            top, bot = t[:half], t[half:]
            store(2 * p, lanes(top[:, :dim], bot[:, :dim]))
            store(2 * p + 1, lanes(top[:, dim:], bot[:, dim:]))

    def x_slot(slot):
        for p in range(n // 2):
            h = slot * n + 2 * p
            if h < heads:
                t = x_ref[0, :, h * dim : (h + 2) * dim]
                top, bot = t[:half], t[half:]
                xs[2 * p, slot] = lanes(top[:, :dim], bot[:, :dim])
                xs[2 * p + 1, slot] = lanes(top[:, dim:], bot[:, dim:])
            else:
                xs[2 * p, slot] = jnp.zeros((half, 2 * dim), BF16)
                xs[2 * p + 1, slot] = jnp.zeros((half, 2 * dim), BF16)
        xr[me, slot] = xs[me, slot]

    def qk_slot():
        for which, src in enumerate((q_ref, k_ref)):
            for p in range(per * n // 2):
                t = src[0, :, p * 2 * dim : (p + 1) * 2 * dim]
                top, bot = t[:half], t[half:]
                h = 2 * p
                qks[h % n, 2 * (h // n) + which] = lanes(top[:, :dim], bot[:, :dim])
                h = 2 * p + 1
                qks[h % n, 2 * (h // n) + which] = lanes(top[:, dim:], bot[:, dim:])
        qkr[me] = qks[me]

    pl.semaphore_wait(barrier, n - 1)
    start(bc_copy)
    start(ld_copy)
    x_slot(0)
    start(x_copy(0))
    qk_slot()
    start(qk_copy)
    for slot in range(1, slots):
        x_slot(slot)
        start(x_copy(slot))

    def unpack(ref, index):
        parts = []
        for c in range(n):
            t = ref[c, index]
            parts += [t[:, :dim], t[:, dim:]]
        return rows(parts)

    def packed(a):
        return lanes(a[:half], a[half:])

    arrive(bc_copy)
    b_all = bcr[:, 0:tok, :].reshape(length, bcr.shape[2])
    for i in range(nblk):
        if blk % tok == 0:
            c_i = bcr[i * (blk // tok) : (i + 1) * (blk // tok), tok:, :].reshape(blk, bcr.shape[2])
        inner[i * blk : (i + 1) * blk, 0 : (i + 1) * blk] = lax.dot_general(
            c_i, b_all[: (i + 1) * blk], (((1,), (1,)), ((), ())), preferred_element_type=F32)
    arrive(ld_copy)
    offset = jnp.zeros((ldr.shape[1], 1), F32)
    parts = []
    for c in range(n):
        part = ldr[c][:, :tok] + offset
        offset = part[:, tok - 1 : tok]
        parts.append(part)
    cum = jnp.concatenate(parts, axis=1)
    cum_t = cum.T

    lower = (lax.broadcasted_iota(jnp.int32, (blk, blk), 0)
             >= lax.broadcasted_iota(jnp.int32, (blk, blk), 1))

    def attend(slot, values):
        q = unpack(qkr, 2 * slot)
        key = unpack(qkr, 2 * slot + 1)
        for i in range(nblk):
            s = lax.dot_general(q[i * blk : (i + 1) * blk], key[: (i + 1) * blk],
                                (((1,), (1,)), ((), ())), preferred_element_type=F32)
            s = s * (dim ** -0.5 * LOG2E)
            diag = jnp.where(lower, s[:, i * blk :], -jnp.inf)
            s = diag if i == 0 else lanes(s[:, : i * blk], diag)
            top = jnp.max(s, axis=-1, keepdims=True)
            w = jnp.exp2(s - top)
            total = jnp.sum(w, axis=-1, keepdims=True)
            mixed = jnp.dot(w.astype(BF16), values[: (i + 1) * blk], preferred_element_type=F32) / total
            mixed = mixed.astype(BF16)
            for c in range(blk // tok):
                ats[i * (blk // tok) + c, slot] = packed(mixed[c * tok : (c + 1) * tok])

    for slot in range(slots):
        head = jnp.minimum(me + slot * n, heads - 1)
        arrive(x_copy(slot))
        x_all = unpack(xr, slot)
        skip = skip_ref[head]
        pair = gain_ref[pl.ds(head // 2, 1), :]
        gain = jnp.where(head % 2 == 0, pair[:, :dim], pair[:, dim:])
        outs = []
        for i in range(nblk):
            here = cum_t[i * blk : (i + 1) * blk, slot : slot + 1]
            w = here - cum[slot : slot + 1, : (i + 1) * blk]
            diag = jnp.where(lower, w[:, i * blk :], -jnp.inf)
            w = diag if i == 0 else lanes(w[:, : i * blk], diag)
            w = jnp.exp2(w) * inner[i * blk : (i + 1) * blk, : (i + 1) * blk]
            y = jnp.dot(w.astype(BF16), x_all[: (i + 1) * blk], preferred_element_type=F32)
            y = y + skip * x_all[i * blk : (i + 1) * blk].astype(F32)
            mean = jnp.mean(y * y, axis=-1, keepdims=True)
            y = (y * lax.rsqrt(mean + 1e-05) * gain).astype(BF16)
            for c in range(blk // tok):
                ys[i * (blk // tok) + c, slot] = packed(y[c * tok : (c + 1) * tok])
            outs.append(y)
        start(y_copy(slot))
        yr[me, slot] = ys[me, slot]
        if slot < per:
            if slot == 0:
                arrive(qk_copy)
            attend(slot, rows(outs))
            if slot == per - 1:
                start(att_copy)
                atr[me] = ats[me]

    def unpack_out(ref, slot, dst):
        for p in range(n // 2):
            h = slot * n + 2 * p
            if h * dim < dst.shape[2]:
                even, odd = ref[2 * p, slot], ref[2 * p + 1, slot]
                dst[0, :half, h * dim : (h + 2) * dim] = lanes(even[:, :dim], odd[:, :dim])
                dst[0, half:, h * dim : (h + 2) * dim] = lanes(even[:, dim:], odd[:, dim:])

    for slot in range(slots):
        arrive(y_copy(slot))
        unpack_out(yr, slot, out_ref)
        if slot == per - 1:
            arrive(att_copy)
            for a in range(per):
                unpack_out(atr, a, att_ref)

    left(bc_copy)
    left(ld_copy)
    left(qk_copy)
    left(att_copy)
    for slot in range(slots):
        left(x_copy(slot))
        left(y_copy(slot))


def local(n, x_in, b_in, c_in, log_decay, skip, norm_gain, queries, keys):
    tok, width = x_in.shape[1:]
    heads = log_decay.shape[1]
    dim = width // heads
    state = b_in.shape[2]
    per = queries.shape[2] // dim // n
    slots = -(-heads // n)
    length = n * tok
    blk = 128 if length <= 512 else 256
    half = tok // 2
    pad = -(-slots // 8) * 8
    vmem = pl.BlockSpec(memory_space=pltpu.VMEM)
    smem = pl.BlockSpec(memory_space=pltpu.SMEM)
    block = lambda k: pltpu.VMEM((n, k, half, 2 * dim), BF16)
    rows_of = FIXED + 2 * slots
    return pl.pallas_call(
        functools.partial(kernel, n, tok, heads, dim, per, blk),
        out_shape=(jax.ShapeDtypeStruct(x_in.shape, BF16), jax.ShapeDtypeStruct(queries.shape, BF16)),
        in_specs=[vmem, vmem, vmem, vmem, smem, vmem, vmem, vmem],
        out_specs=(vmem, vmem),
        scratch_shapes=[
            block(slots), block(slots), block(2 * per), block(2 * per),
            pltpu.VMEM((2 * tok, state), BF16), pltpu.VMEM((n, 2 * tok, state), BF16),
            pltpu.VMEM((n, pad, 128), F32), pltpu.VMEM((n, pad, 128), F32),
            block(slots), block(slots), block(per), block(per),
            pltpu.VMEM((length, length), F32),
            pltpu.SemaphoreType.DMA((rows_of, n)), pltpu.SemaphoreType.DMA((rows_of, n)),
        ],
        compiler_params=pltpu.CompilerParams(
            collective_id=0, has_side_effects=True, vmem_limit_bytes=48 * 1024 * 1024),
    )(x_in, b_in, c_in, log_decay, skip, norm_gain.reshape(width // (2 * dim), 2 * dim), queries, keys)


def solution(mesh):
    rows_spec = P(("groups", "batch"), "seq", None)
    return jax.shard_map(
        functools.partial(local, mesh.shape["seq"]),
        mesh=mesh,
        in_specs=(rows_spec, rows_spec, rows_spec, P(("groups", "batch"), None, "seq"),
                  P(), P(), rows_spec, rows_spec),
        out_specs=(rows_spec, rows_spec),
        check_vma=False,
    )
```

time: 215 us -> 45.5 us (0.21)
  waiting for transfers between devices: 123 us -> 0 us
  Pallas kernels: 0 us -> 36.8 us
  starting transfers between devices: 28 us -> 0 us
  blocking collectives: 22.4 us -> 0 us
  between operations: 15.1 us -> 0.66 us
  matrix products: 7.9 us -> 0 us
  local copies, waits for them, and re-layouts: 13.7 us -> 7.52 us
  other arithmetic: 4.59 us -> 0 us
    all_gather x1 -> x0, waiting for transfers between devices: 106 us -> none  [carried_in(): gathered = jax.tree.map(lambda a: lax.all_gather(a, axis), part)]
    pallas_call x0 -> x1, Pallas kernels: none -> 36.8 us  [local(): pl.pallas_call(functools.partial(kernel, n, tok, heads, dim, per, blk), o...]
    all_to_all x4 -> x0, starting transfers between devices: 28 us -> none  [the longest x1 14 us: local(): lax.all_to_all(values, 'seq', split_axis=1, concat_axis=0, tiled=True)]
    unnamed x1 -> x0, blocking collectives: 22.4 us -> none
    all_to_all x4 -> x0, waiting for transfers between devices: 17.2 us -> none  [the longest x1 7.29 us: local(): lax.all_to_all(keys[0], 'seq', split_axis=1, concat_axis=0, tiled=True)]
    dot_general x7 -> x0, matrix products: 7.9 us -> none  [the longest x1 1.87 us: advance(): fresh = jnp.einsum('hs,shp,sn->hpn', tail, xs, bs, precision=HIGH)]
    unnamed x41 -> x18, local copies, waits for them, and re-layouts: 6.65 us -> 7.52 us
  transfers between devices with their start and end apart: 5 -> 0, of which waited for: 4 -> 0; matrix products, arithmetic and copies ran while one was open for 6% -> 0% of each run, Pallas kernels for 0% -> 0%
where the time goes in v1:
time: 45.5 us; the launch traced here: 45 us
  Pallas kernels  36.8 us (81%)
  local copies, waits for them, and re-layouts  7.52 us (17%)
  between operations  0.66 us (1%)
    pallas_call x1, Pallas kernels, local(): pl.pallas_call(functools.partial(kernel, n, tok, heads, dim, per, blk), o...  36.8 us
    unnamed x18, local copies, waits for them, and re-layouts  7.52 us

profile of v1, /device:TPU:0, one launch (start us, length us, event | category | flops | bytes accessed | tf_op | source)
XLA Modules:
  0.0 45.0 jit_solution(8179704471433389342)
XLA Ops:
  0.6 0.0 copy-start.7
  0.6 0.6 %copy-done.7 = f32[40]{0:T(128)S(1)} copy-done((f32[40]{0:T(128)S(1)}, f32[40]{0:T(128)}, u32[]{:S(2)}) %copy-start.7) | copy-done | bytes 184
  1.3 0.0 copy-start
  1.3 1.0 %copy-done = bf16[1,64,2560]{2,1,0:T(8,128)(2,1)S(1)} copy-done((bf16[1,64,2560]{2,1,0:T(8,128)(2,1)S(1)}, bf16[1,64,2560]{2,1,0:T(8,128)(2,1)}, u32[]{:S(2)}) %copy-start) | copy-done | bytes 327704
  2.3 0.0 copy-start.1
  2.3 0.8 %copy-done.1 = bf16[1,64,512]{2,1,0:T(8,128)(2,1)S(1)} copy-done((bf16[1,64,512]{2,1,0:T(8,128)(2,1)S(1)}, bf16[1,64,512]{2,1,0:T(8,128)(2,1)}, u32[]{:S(2)}) %copy-start.1) | copy-done | bytes 65560
  3.1 0.0 copy-start.2
  3.1 0.8 %copy-done.2 = bf16[1,64,512]{2,1,0:T(8,128)(2,1)S(1)} copy-done((bf16[1,64,512]{2,1,0:T(8,128)(2,1)S(1)}, bf16[1,64,512]{2,1,0:T(8,128)(2,1)}, u32[]{:S(2)}) %copy-start.2) | copy-done | bytes 65560
  3.9 0.0 copy-start.3
  3.9 0.7 %copy-done.3 = f32[1,40,64]{2,1,0:T(8,128)S(1)} copy-done((f32[1,40,64]{2,1,0:T(8,128)S(1)}, f32[1,40,64]{2,1,0:T(8,128)}, u32[]{:S(2)}) %copy-start.3) | copy-done | bytes 10264
  4.7 0.0 copy-start.4
  4.7 0.7 %copy-done.4 = bf16[1,64,128]{2,1,0:T(8,128)(2,1)S(1)} copy-done((bf16[1,64,128]{2,1,0:T(8,128)(2,1)S(1)}, bf16[1,64,128]{2,1,0:T(8,128)(2,1)}, u32[]{:S(2)}) %copy-start.4) | copy-done | bytes 16408
  5.4 0.0 copy-start.5
  5.4 0.7 %copy-done.5 = bf16[1,64,128]{2,1,0:T(8,128)(2,1)S(1)} copy-done((bf16[1,64,128]{2,1,0:T(8,128)(2,1)S(1)}, bf16[1,64,128]{2,1,0:T(8,128)(2,1)}, u32[]{:S(2)}) %copy-start.5) | copy-done | bytes 16408
  6.1 0.0 copy-start.6
  6.1 0.7 %copy-done.6 = f32[2560]{0:T(1024)S(1)} copy-done((f32[2560]{0:T(1024)S(1)}, f32[2560]{0:T(1024)}, u32[]{:S(2)}) %copy-start.6) | copy-done | bytes 10264
  6.8 36.8 %shard_map.95 = (bf16[1,64,2560]{2,1,0:T(8,128)(2,1)S(1)}, bf16[1,64,512]{2,1,0:T(8,128)(2,1)S(1)}) custom-call(bf16[1,64,2560]{2,1,0:T(8,128)(2,1)S(1)} %copy-done, bf16[1,64,128]{2,1,0:T(8,128)(2,1)S(1)} %copy-done.4, bf16[1,64,128]{2,1,0:T(8,128)(2,1)S(1)} %copy-done.5, f32[1,40,64]{2,1,0:T(8,128)S(1)} %copy-done.3, f32[40]{0:T(128)S(1)} %copy-done.7, ...), custom_call_target="tpu_custom_call" | custom-call | tf_op jit(solution)/shard_map/pallas_call | solution.py:240
  43.7 0.7 %copy.12 = bf16[1,64,2560]{2,1,0:T(8,128)(2,1)} copy(bf16[1,64,2560]{2,1,0:T(8,128)(2,1)S(1)} %get-tuple-element.4) | data formatting | bytes 655360
  44.4 0.6 %copy.13 = bf16[1,64,512]{2,1,0:T(8,128)(2,1)} copy(bf16[1,64,512]{2,1,0:T(8,128)(2,1)S(1)} %get-tuple-element.5) | data formatting | bytes 131072
Async XLA Ops:
  0.6 0.7 %copy-start.7 = (f32[40]{0:T(128)S(1)}, f32[40]{0:T(128)}, u32[]{:S(2)}) copy-start(f32[40]{0:T(128)} %skip_ref.1) | copy-start | bytes 484
  1.3 1.0 %copy-start = (bf16[1,64,2560]{2,1,0:T(8,128)(2,1)S(1)}, bf16[1,64,2560]{2,1,0:T(8,128)(2,1)}, u32[]{:S(2)}) copy-start(bf16[1,64,2560]{2,1,0:T(8,128)(2,1)} %x_ref.1) | copy-start | bytes 983044
  2.3 0.8 %copy-start.1 = (bf16[1,64,512]{2,1,0:T(8,128)(2,1)S(1)}, bf16[1,64,512]{2,1,0:T(8,128)(2,1)}, u32[]{:S(2)}) copy-start(bf16[1,64,512]{2,1,0:T(8,128)(2,1)} %q_ref.1) | copy-start | bytes 196612
  3.1 0.8 %copy-start.2 = (bf16[1,64,512]{2,1,0:T(8,128)(2,1)S(1)}, bf16[1,64,512]{2,1,0:T(8,128)(2,1)}, u32[]{:S(2)}) copy-start(bf16[1,64,512]{2,1,0:T(8,128)(2,1)} %k_ref.1) | copy-start | bytes 196612
  3.9 0.7 %copy-start.3 = (f32[1,40,64]{2,1,0:T(8,128)S(1)}, f32[1,40,64]{2,1,0:T(8,128)}, u32[]{:S(2)}) copy-start(f32[1,40,64]{2,1,0:T(8,128)} %ld_ref.1) | copy-start | bytes 30724
  4.7 0.7 %copy-start.4 = (bf16[1,64,128]{2,1,0:T(8,128)(2,1)S(1)}, bf16[1,64,128]{2,1,0:T(8,128)(2,1)}, u32[]{:S(2)}) copy-start(bf16[1,64,128]{2,1,0:T(8,128)(2,1)} %b_ref.1) | copy-start | bytes 49156
  5.4 0.7 %copy-start.5 = (bf16[1,64,128]{2,1,0:T(8,128)(2,1)S(1)}, bf16[1,64,128]{2,1,0:T(8,128)(2,1)}, u32[]{:S(2)}) copy-start(bf16[1,64,128]{2,1,0:T(8,128)(2,1)} %c_ref.1) | copy-start | bytes 49156
  6.1 0.7 %copy-start.6 = (f32[2560]{0:T(1024)S(1)}, f32[2560]{0:T(1024)}, u32[]{:S(2)}) copy-start(f32[2560]{0:T(1024)} %param.13) | copy-start | bytes 30724

commit v2 on v1

--- a/solution.py
+++ b/solution.py
@@ -12,7 +12,7 @@
 HIGH = lax.Precision.HIGHEST
 LOG2E = math.log2(math.e)
 MESH = pl.DeviceIdType.MESH
-BC, LD, QK, ATT, FIXED = 0, 1, 2, 3, 4
+BC, LD, QK, ATT, FWD, FIXED = 0, 1, 2, 3, 4, 5
 
 
 def lanes(a, b):
@@ -24,15 +24,20 @@
 
 
 def kernel(n, tok, heads, dim, per, blk,
-           x_ref, b_ref, c_ref, ld_ref, skip_ref, gain_ref, q_ref, k_ref,
+           x_hbm, b_hbm, c_hbm, ld_hbm, skip_ref, gain_hbm, q_hbm, k_hbm,
            out_ref, att_ref,
-           xs, xr, qks, qkr, bcs, bcr, lds, ldr, ys, yr, ats, atr, inner, send, recv):
+           x_ref, ld_ref, gain_ref, q_ref, k_ref, load, xs, xr, qks, qkr, bcs, bcr, lds, ldr, ys, yr, ats, atr, inner, send, recv):
     me = lax.axis_index("seq")
     half = tok // 2
     slots = xs.shape[1]
     length = n * tok
     nblk = length // blk
 
+    loads = [pltpu.make_async_copy(src, dst, load.at[i]) for i, (src, dst) in enumerate((
+        (b_hbm.at[0], bcs.at[0:tok]), (c_hbm.at[0], bcs.at[tok : 2 * tok]), (ld_hbm, ld_ref), (x_hbm, x_ref),
+        (q_hbm, q_ref), (k_hbm, k_ref), (gain_hbm, gain_ref)))]
+    for one in loads:
+        one.start()
     barrier = pltpu.get_barrier_semaphore()
 
     def greet(k, _):
@@ -54,6 +59,29 @@
             fn(k)
             return 0
         lax.fori_loop(1, n, body, 0)
+
+    partner = me + 1 - 2 * lax.rem(me, 2)
+
+    def bc_partner():
+        return pltpu.make_async_remote_copy(
+            src_ref=bcs, dst_ref=bcr.at[me], send_sem=send.at[BC, 1], recv_sem=recv.at[BC, 1],
+            device_id={"seq": partner}, device_id_type=MESH)
+
+    def bc_forward(k):
+        slot = lax.rem(me + n - k, n)
+        return pltpu.make_async_remote_copy(
+            src_ref=bcr.at[slot], dst_ref=bcr.at[slot], send_sem=send.at[FWD, k], recv_sem=recv.at[FWD, k],
+            device_id={"seq": partner}, device_id_type=MESH)
+
+    def evens(fn):
+        def body(j, _):
+            fn(2 * j)
+            return 0
+        lax.fori_loop(1, n // 2, body, 0)
+
+    def bc_relay(k):
+        bc_copy(k).wait_recv()
+        bc_forward(k).start()
 
     bc_copy = lambda k: copy(bcs, bcr.at[me], BC, k)
     ld_copy = lambda k: copy(lds.at[to(k)], ldr.at[me], LD, k)
@@ -65,24 +93,17 @@
     arrive = lambda mk: each(lambda k: mk(k).wait_recv())
     left = lambda mk: each(lambda k: mk(k).wait_send())
 
-    bcs[0:tok] = b_ref[0]
-    bcs[tok:] = c_ref[0]
+    lds[...] = jnp.zeros_like(lds)
+    for one in loads[:3]:
+        one.wait()
     bcr[me] = bcs[...]
     upper = (lax.broadcasted_iota(jnp.int32, (tok, tok), 0)
              <= lax.broadcasted_iota(jnp.int32, (tok, tok), 1)).astype(F32)
     sums = jnp.dot(ld_ref[0], upper, precision=HIGH, preferred_element_type=F32) * LOG2E
-    lds[...] = jnp.zeros_like(lds)
     for slot in range(slots):
         count = min(n, heads - slot * n)
         lds[0:count, slot, 0:tok] = sums[slot * n : slot * n + count]
     ldr[me] = lds[me]
-
-    def pack(src, head_of, store):
-        for p in range(src.shape[2] // (2 * dim)):
-            t = src[0, :, p * 2 * dim : (p + 1) * 2 * dim]
-            top, bot = t[:half], t[half:]
-            store(2 * p, lanes(top[:, :dim], bot[:, :dim]))
-            store(2 * p + 1, lanes(top[:, dim:], bot[:, dim:]))
 
     def x_slot(slot):
         for p in range(n // 2):
@@ -108,13 +129,18 @@
                 qks[h % n, 2 * (h // n) + which] = lanes(top[:, dim:], bot[:, dim:])
         qkr[me] = qks[me]
 
+    loads[3].wait()
+    x_slot(0)
     pl.semaphore_wait(barrier, n - 1)
-    start(bc_copy)
+    evens(lambda k: bc_copy(k).start())
+    bc_partner().start()
     start(ld_copy)
-    x_slot(0)
     start(x_copy(0))
+    loads[4].wait()
+    loads[5].wait()
     qk_slot()
     start(qk_copy)
+    evens(bc_relay)
     for slot in range(1, slots):
         x_slot(slot)
         start(x_copy(slot))
@@ -129,7 +155,8 @@
     def packed(a):
         return lanes(a[:half], a[half:])
 
-    arrive(bc_copy)
+    bc_partner().wait_recv()
+    evens(lambda k: bc_forward(k).wait_recv())
     b_all = bcr[:, 0:tok, :].reshape(length, bcr.shape[2])
     for i in range(nblk):
         if blk % tok == 0:
@@ -145,6 +172,7 @@
         parts.append(part)
     cum = jnp.concatenate(parts, axis=1)
     cum_t = cum.T
+    loads[6].wait()
 
     lower = (lax.broadcasted_iota(jnp.int32, (blk, blk), 0)
              >= lax.broadcasted_iota(jnp.int32, (blk, blk), 1))
@@ -213,7 +241,9 @@
             for a in range(per):
                 unpack_out(atr, a, att_ref)
 
-    left(bc_copy)
+    bc_partner().wait_send()
+    evens(lambda k: bc_copy(k).wait_send())
+    evens(lambda k: bc_forward(k).wait_send())
     left(ld_copy)
     left(qk_copy)
     left(att_copy)
@@ -234,15 +264,19 @@
     half = tok // 2
     pad = -(-slots // 8) * 8
     vmem = pl.BlockSpec(memory_space=pltpu.VMEM)
+    hbm = pl.BlockSpec(memory_space=pltpu.HBM)
     smem = pl.BlockSpec(memory_space=pltpu.SMEM)
     block = lambda k: pltpu.VMEM((n, k, half, 2 * dim), BF16)
     rows_of = FIXED + 2 * slots
     return pl.pallas_call(
         functools.partial(kernel, n, tok, heads, dim, per, blk),
         out_shape=(jax.ShapeDtypeStruct(x_in.shape, BF16), jax.ShapeDtypeStruct(queries.shape, BF16)),
-        in_specs=[vmem, vmem, vmem, vmem, smem, vmem, vmem, vmem],
+        in_specs=[hbm, hbm, hbm, hbm, smem, hbm, hbm, hbm],
         out_specs=(vmem, vmem),
         scratch_shapes=[
+            pltpu.VMEM(x_in.shape, BF16), pltpu.VMEM(log_decay.shape, F32),
+            pltpu.VMEM((width // (2 * dim), 2 * dim), F32), pltpu.VMEM(queries.shape, BF16),
+            pltpu.VMEM(keys.shape, BF16), pltpu.SemaphoreType.DMA((7,)),
             block(slots), block(slots), block(2 * per), block(2 * per),
             pltpu.VMEM((2 * tok, state), BF16), pltpu.VMEM((n, 2 * tok, state), BF16),
             pltpu.VMEM((n, pad, 128), F32), pltpu.VMEM((n, pad, 128), F32),
@@ -251,7 +285,7 @@
             pltpu.SemaphoreType.DMA((rows_of, n)), pltpu.SemaphoreType.DMA((rows_of, n)),
         ],
         compiler_params=pltpu.CompilerParams(
-            collective_id=0, has_side_effects=True, vmem_limit_bytes=48 * 1024 * 1024),
+            collective_id=0, has_side_effects=True, vmem_limit_bytes=63 * 1024 * 1024),
     )(x_in, b_in, c_in, log_decay, skip, norm_gain.reshape(width // (2 * dim), 2 * dim), queries, keys)
 
 

time: 45.5 us -> 38.4 us (0.84)
  local copies, waits for them, and re-layouts: 7.52 us -> 2.38 us
  Pallas kernels: 36.8 us -> 35.1 us
    unnamed x18 -> x4, local copies, waits for them, and re-layouts: 7.52 us -> 2.38 us
    pallas_call x1, Pallas kernels: 36.8 us -> 35.1 us  [local(): pl.pallas_call(functools.partial(kernel, n, tok, heads, dim, per, blk), o...]
where the time goes in v2:
time: 38.4 us; the launch traced here: 38.2 us
  Pallas kernels  35.1 us (91%)
  local copies, waits for them, and re-layouts  2.38 us (6%)
  between operations  0.65 us (2%)
    pallas_call x1, Pallas kernels, local(): pl.pallas_call(functools.partial(kernel, n, tok, heads, dim, per, blk), o...  35.1 us
    unnamed x4, local copies, waits for them, and re-layouts  2.38 us

profile of v2, /device:TPU:0, one launch (start us, length us, event | category | flops | bytes accessed | tf_op | source)
XLA Modules:
  0.0 38.2 jit_solution(7999080457223331857)
XLA Ops:
  0.6 35.1 %shard_map.95 = (bf16[1,64,2560]{2,1,0:T(8,128)(2,1)}, bf16[1,64,512]{2,1,0:T(8,128)(2,1)}) custom-call(bf16[1,64,2560]{2,1,0:T(8,128)(2,1)} %x_hbm.1, bf16[1,64,128]{2,1,0:T(8,128)(2,1)} %b_hbm.1, bf16[1,64,128]{2,1,0:T(8,128)(2,1)} %c_hbm.1, f32[1,40,64]{2,1,0:T(8,128)} %ld_hbm.1, f32[40]{0:T(128)} %skip_ref.1, f32[20,128]{1,0:T(8,128)} %bitcast.1, ...), custom_call_target="tpu_custom_call" | custom-call | tf_op jit(solution)/shard_map/pallas_call | solution.py:271
  35.8 0.0 copy-start
  35.8 1.7 %copy.12 = bf16[1,64,2560]{2,1,0:T(8,128)(2,1)} copy(bf16[1,64,2560]{2,1,0:T(8,128)(2,1)} %get-tuple-element.4) | data formatting | bytes 655360
  37.5 0.0 copy-done
  37.5 0.6 %copy.13 = bf16[1,64,512]{2,1,0:T(8,128)(2,1)} copy(bf16[1,64,512]{2,1,0:T(8,128)(2,1)S(1)} %copy-done) | data formatting | bytes 131072
Async XLA Ops:
  35.8 1.8 %copy-start = (bf16[1,64,512]{2,1,0:T(8,128)(2,1)S(1)}, bf16[1,64,512]{2,1,0:T(8,128)(2,1)}, u32[]{:S(2)}) copy-start(bf16[1,64,512]{2,1,0:T(8,128)(2,1)} %get-tuple-element.5) | copy-start | bytes 196612

commit v3 on v2

--- a/solution.py
+++ b/solution.py
@@ -89,22 +89,11 @@
     att_copy = lambda k: copy(ats.at[to(k)], atr.at[me], ATT, k)
     x_copy = lambda slot: lambda k: copy(xs.at[to(k), slot], xr.at[me, slot], FIXED + slot, k)
     y_copy = lambda slot: lambda k: copy(ys.at[to(k), slot], yr.at[me, slot], FIXED + slots + slot, k)
-    start = lambda mk: each(lambda k: mk(k).start())
+    start = lambda mk: each(lambda k: mk(n - k).start())
     arrive = lambda mk: each(lambda k: mk(k).wait_recv())
     left = lambda mk: each(lambda k: mk(k).wait_send())
 
     lds[...] = jnp.zeros_like(lds)
-    for one in loads[:3]:
-        one.wait()
-    bcr[me] = bcs[...]
-    upper = (lax.broadcasted_iota(jnp.int32, (tok, tok), 0)
-             <= lax.broadcasted_iota(jnp.int32, (tok, tok), 1)).astype(F32)
-    sums = jnp.dot(ld_ref[0], upper, precision=HIGH, preferred_element_type=F32) * LOG2E
-    for slot in range(slots):
-        count = min(n, heads - slot * n)
-        lds[0:count, slot, 0:tok] = sums[slot * n : slot * n + count]
-    ldr[me] = lds[me]
-
     def x_slot(slot):
         for p in range(n // 2):
             h = slot * n + 2 * p
@@ -131,11 +120,23 @@
 
     loads[3].wait()
     x_slot(0)
+    loads[0].wait()
+    loads[1].wait()
     pl.semaphore_wait(barrier, n - 1)
-    evens(lambda k: bc_copy(k).start())
+    evens(lambda k: bc_copy(n - k).start())
     bc_partner().start()
+    start(x_copy(0))
+    bcr[me] = bcs[...]
+    loads[2].wait()
+    upper = (lax.broadcasted_iota(jnp.int32, (tok, tok), 0)
+             <= lax.broadcasted_iota(jnp.int32, (tok, tok), 1)).astype(F32)
+    sums = jnp.dot(ld_ref[0], upper, precision=HIGH, preferred_element_type=F32) * LOG2E
+    for slot in range(slots):
+        count = min(n, heads - slot * n)
+        lds[0:count, slot, 0:tok] = sums[slot * n : slot * n + count]
+    ldr[me] = lds[me]
+
     start(ld_copy)
-    start(x_copy(0))
     loads[4].wait()
     loads[5].wait()
     qk_slot()

time: 38.4 us -> 36.4 us (0.948)
  Pallas kernels: 35.1 us -> 33.2 us
    pallas_call x1, Pallas kernels: 35.1 us -> 33.2 us  [local(): pl.pallas_call(functools.partial(kernel, n, tok, heads, dim, per, blk), o...]
where the time goes in v3:
time: 36.4 us; the launch traced here: 36.3 us
  Pallas kernels  33.2 us (91%)
  local copies, waits for them, and re-layouts  2.38 us (7%)
  between operations  0.65 us (2%)
    pallas_call x1, Pallas kernels, local(): pl.pallas_call(functools.partial(kernel, n, tok, heads, dim, per, blk), o...  33.2 us
    unnamed x4, local copies, waits for them, and re-layouts  2.38 us

profile of v3, /device:TPU:0, one launch (start us, length us, event | category | flops | bytes accessed | tf_op | source)
XLA Modules:
  0.0 36.3 jit_solution(14769728402281245757)
XLA Ops:
  0.6 33.2 %shard_map.95 = (bf16[1,64,2560]{2,1,0:T(8,128)(2,1)}, bf16[1,64,512]{2,1,0:T(8,128)(2,1)}) custom-call(bf16[1,64,2560]{2,1,0:T(8,128)(2,1)} %x_hbm.1, bf16[1,64,128]{2,1,0:T(8,128)(2,1)} %b_hbm.1, bf16[1,64,128]{2,1,0:T(8,128)(2,1)} %c_hbm.1, f32[1,40,64]{2,1,0:T(8,128)} %ld_hbm.1, f32[40]{0:T(128)} %skip_ref.1, f32[20,128]{1,0:T(8,128)} %bitcast.1, ...), custom_call_target="tpu_custom_call" | custom-call | tf_op jit(solution)/shard_map/pallas_call | solution.py:272
  33.9 0.0 copy-start
  33.9 1.7 %copy.12 = bf16[1,64,2560]{2,1,0:T(8,128)(2,1)} copy(bf16[1,64,2560]{2,1,0:T(8,128)(2,1)} %get-tuple-element.4) | data formatting | bytes 655360
  35.6 0.0 copy-done
  35.6 0.6 %copy.13 = bf16[1,64,512]{2,1,0:T(8,128)(2,1)} copy(bf16[1,64,512]{2,1,0:T(8,128)(2,1)S(1)} %copy-done) | data formatting | bytes 131072
Async XLA Ops:
  33.9 1.8 %copy-start = (bf16[1,64,512]{2,1,0:T(8,128)(2,1)S(1)}, bf16[1,64,512]{2,1,0:T(8,128)(2,1)}, u32[]{:S(2)}) copy-start(bf16[1,64,512]{2,1,0:T(8,128)(2,1)} %get-tuple-element.5) | copy-start | bytes 196612

commit v4 on v3

--- a/solution.py
+++ b/solution.py
@@ -58,7 +58,7 @@
         def body(k, _):
             fn(k)
             return 0
-        lax.fori_loop(1, n, body, 0)
+        lax.fori_loop(1, n, body, 0, unroll=n <= 8)
 
     partner = me + 1 - 2 * lax.rem(me, 2)
 
@@ -77,7 +77,7 @@
         def body(j, _):
             fn(2 * j)
             return 0
-        lax.fori_loop(1, n // 2, body, 0)
+        lax.fori_loop(1, n // 2, body, 0, unroll=n <= 8)
 
     def bc_relay(k):
         bc_copy(k).wait_recv()

time: 36.4 us -> 35.9 us (0.986)
  Pallas kernels: 33.2 us -> 32.7 us
    pallas_call x1, Pallas kernels: 33.2 us -> 32.7 us  [local(): pl.pallas_call(functools.partial(kernel, n, tok, heads, dim, per, blk), o...]
where the time goes in v4:
time: 35.9 us; the launch traced here: 35.7 us
  Pallas kernels  32.7 us (91%)
  local copies, waits for them, and re-layouts  2.38 us (7%)
  between operations  0.65 us (2%)
    pallas_call x1, Pallas kernels, local(): pl.pallas_call(functools.partial(kernel, n, tok, heads, dim, per, blk), o...  32.7 us
    unnamed x4, local copies, waits for them, and re-layouts  2.38 us

profile of v4, /device:TPU:0, one launch (start us, length us, event | category | flops | bytes accessed | tf_op | source)
XLA Modules:
  0.0 35.7 jit_solution(8547438557435895867)
XLA Ops:
  0.6 32.7 %shard_map.95 = (bf16[1,64,2560]{2,1,0:T(8,128)(2,1)}, bf16[1,64,512]{2,1,0:T(8,128)(2,1)}) custom-call(bf16[1,64,2560]{2,1,0:T(8,128)(2,1)} %x_hbm.1, bf16[1,64,128]{2,1,0:T(8,128)(2,1)} %b_hbm.1, bf16[1,64,128]{2,1,0:T(8,128)(2,1)} %c_hbm.1, f32[1,40,64]{2,1,0:T(8,128)} %ld_hbm.1, f32[40]{0:T(128)} %skip_ref.1, f32[20,128]{1,0:T(8,128)} %bitcast.1, ...), custom_call_target="tpu_custom_call" | custom-call | tf_op jit(solution)/shard_map/pallas_call | solution.py:272
  33.4 0.0 copy-start
  33.4 1.7 %copy.12 = bf16[1,64,2560]{2,1,0:T(8,128)(2,1)} copy(bf16[1,64,2560]{2,1,0:T(8,128)(2,1)} %get-tuple-element.4) | data formatting | bytes 655360
  35.1 0.0 copy-done
  35.1 0.6 %copy.13 = bf16[1,64,512]{2,1,0:T(8,128)(2,1)} copy(bf16[1,64,512]{2,1,0:T(8,128)(2,1)S(1)} %copy-done) | data formatting | bytes 131072
Async XLA Ops:
  33.4 1.8 %copy-start = (bf16[1,64,512]{2,1,0:T(8,128)(2,1)S(1)}, bf16[1,64,512]{2,1,0:T(8,128)(2,1)}, u32[]{:S(2)}) copy-start(bf16[1,64,512]{2,1,0:T(8,128)(2,1)} %get-tuple-element.5) | copy-start | bytes 196612
